TPU v7x, 32 devices: a whole 2x2x4 slice. The times are simulated.
32 devices in a mesh: grp: 2 (over x), len: 16 (over z, y, core).
Axes of the slice: x: 2, y: 2, z: 4, core: 2. Of those that a mesh axis runs over, the one named last changes fastest.
Arguments:
- tin_temp: float32 [64, 512, 1024], P(None, ('grp', 'len')), parts along dimension 1, may hold values from -6 to 6
- flow_code: int32 [64, 512, 1024], P(None, ('grp', 'len')), parts along dimension 1, may hold values from 0 to 3
- speeds: float32 [2, 64], replicated, may hold values from 0.02 to 0.12
- floor_temp: float32 [32, 48, 64, 256], P(('grp', 'len')), parts along dimension 0, may hold values from -6 to 6
- material: int32 [32, 48, 64, 256], P(('grp', 'len')), parts along dimension 0, may hold values from 0 to 2
- conductivity: float32 [3], replicated, may hold values from 0.03 to 0.15
Outputs:
- tin_out: float32 [64, 512, 1024], P(None, ('grp', 'len')), parts along dimension 1
- floor_out: float32 [32, 48, 64, 256], P(('grp', 'len')), parts along dimension 0
There are 2 independent parts, one for each index of `grp`. A program takes and returns all parts, laid end to end along the dimension named above; an argument that names none is the same for every part. Nothing has to cross between parts.
Inputs may be any that keep to these rules, and one draw needn't show every extreme that they name: flow_code % 2 is 0 where the tin cell takes its length upwind value from the lower length index and 1 from the higher; flow_code // 2 likewise across the width. material ids index conductivity.
All inputs are finite; a program needn't handle non-finite values.
Results may differ from a plain program's by a relative error of at most 0.0003.
Values sent between devices are 32-bit elements; how exact they have to be, the bound alone decides.
A program may use at most 128 MiB of HBM per device.

v0:
```python
import functools

import jax
import jax.numpy as jnp
from jax import lax
from jax.experimental import pallas as pl
from jax.experimental.pallas import tpu as pltpu
from jax.sharding import PartitionSpec as P

KT = 0.1
HT = 0.2
HR = 0.2
L = 128
S = 8


def kernel(n, ty, tin_h, flow_h, speeds, floor_h, mat_h, cond,
           tin_o, floor_o,
           tin0, flow, tin1, floor0, mat, floor1, kh, kx, ky, kz,
           tlo, thi, tlo_s, thi_s,
           rlo, rhi, rlo_s, rhi_s,
           clo, chi, clo_s, chi_s,
           pp, bb, load_sem, send_sem, recv_sem):
    Z, R, NYW = tin_h.shape
    ZF, CX, CY = floor_h.shape
    me = lax.axis_index("len")
    c = lax.rem(me, ty)
    base = me - c
    up_ok, dn_ok = me < n - 1, me > 0
    rup_ok, rdn_ok = me + ty < n, me >= ty
    cup_ok, cdn_ok = c < ty - 1, c > 0

    loads = [pltpu.make_async_copy(a, b, load_sem.at[i]) for i, (a, b) in enumerate(
        [(tin_h, tin0), (mat_h, mat), (floor_h, floor0), (flow_h, flow)])]
    for ld in loads:
        ld.start()

    barrier = pltpu.get_barrier_semaphore()

    def hello(target):
        pl.semaphore_signal(barrier, inc=1, device_id={"len": target},
                            device_id_type=pl.DeviceIdType.MESH)

    for d in range(1, ty):
        hello(base + lax.rem(c + d, ty))
    pairs = [(rup_ok, me + ty), (rdn_ok, me - ty),
             (jnp.logical_and(c == ty - 1, up_ok), me + 1),
             (jnp.logical_and(c == 0, dn_ok), me - 1)]
    for ok, target in pairs:
        @pl.when(ok)
        def _():
            hello(target)

    row = lax.broadcasted_iota(jnp.int32, (S, L), 0)
    lane = lax.broadcasted_iota(jnp.int32, (S, L), 1)
    row_first, row_last = row == 0, row == S - 1
    lane_first, lane_last = lane == 0, lane == L - 1

    own_p = pltpu.make_async_copy(
        floor_h.at[0, pl.ds(pl.multiple_of(c * R, R), R), :],
        pp.at[0, :, pl.ds(pl.multiple_of(c * CY, CY), CY)], load_sem.at[4])
    own_b = pltpu.make_async_copy(
        tin_h.at[0, :, pl.ds(pl.multiple_of(c * CY, CY), CY)],
        bb.at[0, pl.ds(pl.multiple_of(c * R, R), R), :], load_sem.at[5])
    own_p.start()
    own_b.start()

    def remote(e, slot, src, dst, target):
        return pltpu.make_async_remote_copy(
            src_ref=src, dst_ref=dst, send_sem=send_sem.at[e, slot],
            recv_sem=recv_sem.at[e, slot], device_id={"len": target},
            device_id_type=pl.DeviceIdType.MESH)

    def tin_msgs(e):
        return [(up_ok, dn_ok, remote(e, 0, thi_s.at[e], tlo.at[e], me + 1), tlo),
                (dn_ok, up_ok, remote(e, 1, tlo_s.at[e], thi.at[e], me - 1), thi)]

    def floor_msgs(e):
        if e == 0:
            return [
                (rup_ok, rdn_ok, remote(0, 2, rhi_s.at[0:2], rlo.at[0:2], me + ty), rlo),
                (rdn_ok, rup_ok, remote(0, 3, rlo_s.at[0:2], rhi.at[0:2], me - ty), rhi),
                (cup_ok, cdn_ok, remote(0, 4, chi_s.at[0:2], clo.at[0:2], me + 1), clo),
                (cdn_ok, cup_ok, remote(0, 5, clo_s.at[0:2], chi.at[0:2], me - 1), chi)]
        return [
            (rup_ok, rdn_ok, remote(1, 2, rhi_s.at[2], rlo.at[2], me + ty), rlo),
            (rdn_ok, rup_ok, remote(1, 3, rlo_s.at[2], rhi.at[2], me - ty), rhi),
            (cup_ok, cdn_ok, remote(1, 4, chi_s.at[2], clo.at[2], me + 1), clo),
            (cdn_ok, cup_ok, remote(1, 5, clo_s.at[2], chi.at[2], me - 1), chi)]

    def p_msgs(e, field):
        out = []
        for d in range(1, ty):
            t = lax.rem(c + d, ty)
            out.append(remote(
                e, 5 + d, field.at[0, pl.ds(pl.multiple_of(t * R, R), R), :],
                pp.at[e, :, pl.ds(pl.multiple_of(c * CY, CY), CY)], base + t))
        return out

    def b_msgs(e, field):
        out = []
        for d in range(1, ty):
            t = lax.rem(c + d, ty)
            out.append(remote(
                e, 8 + d, field.at[0, :, pl.ds(pl.multiple_of(t * CY, CY), CY)],
                bb.at[e, pl.ds(pl.multiple_of(c * R, R), R), :], base + t))
        return out

    def start_if(msgs):
        for ok, _, m, _ in msgs:
            @pl.when(ok)
            def _():
                m.start()

    def wait_recv_if(msgs):
        for _, ok, m, _ in msgs:
            @pl.when(ok)
            def _():
                m.wait_recv()

    def wait_send_if(msgs):
        for ok, _, m, _ in msgs:
            @pl.when(ok)
            def _():
                m.wait_send()

    def tile(ref, z, i, j):
        return ref[z, pl.ds(i * S, S), pl.ds(j * L, L)]

    for _, ok, _, buf in tin_msgs(0) + floor_msgs(0):
        @pl.when(jnp.logical_not(ok))
        def _():
            buf[...] = jnp.zeros_like(buf)

    loads[0].wait()

    def pack_tin(z, carry):
        tlo_s[0, pl.ds(z, 1), :] = tin0[z, 0:1, :]
        thi_s[0, pl.ds(z, 1), :] = tin0[z, R - 1:R, :]
        return carry

    lax.fori_loop(0, Z, pack_tin, 0, unroll=4)

    peers = ty - 1
    for ok, _ in pairs:
        peers = peers + ok.astype(jnp.int32)
    pl.semaphore_wait(barrier, peers)

    t0, f0 = tin_msgs(0), floor_msgs(0)
    p0, b0 = p_msgs(0, floor_h), b_msgs(0, tin_h)
    start_if(t0)
    for m in b0 + p0:
        m.start()

    loads[1].wait()
    c0, c1, c2 = cond[0] * 0.5, cond[1] * 0.5, cond[2] * 0.5
    NI, NJ = CX // S, CY // L

    def pack_cols(z, edge_lo, edge_hi, acc):
        lo_acc, hi_acc = acc
        here = lane == z
        lo_n = tuple(jnp.where(here, pltpu.roll(edge_lo[i], z, 1), lo_acc[i]) for i in range(NI))
        hi_n = tuple(jnp.where(here, pltpu.roll(edge_hi[i], z + 1, 1), hi_acc[i]) for i in range(NI))
        return lo_n, hi_n

    def zeros():
        zero = jnp.zeros((S, L), jnp.float32)
        return tuple(zero for _ in range(NI)), tuple(zero for _ in range(NI))

    def store_cols(slot, acc):
        for i in range(NI):
            clo_s[slot, pl.ds(i * S, S), :] = acc[0][i]
            chi_s[slot, pl.ds(i * S, S), :] = acc[1][i]

    def k_layer(z, acc):
        t = {}
        for i in range(NI):
            for j in range(NJ):
                m = tile(mat, z, i, j)
                v = jnp.where(m == 0, c0, jnp.where(m == 1, c1, c2))
                kh[z, pl.ds(i * S, S), pl.ds(j * L, L)] = v
                t[i, j] = v
        rlo_s[1, pl.ds(z, 1), :] = jnp.concatenate([t[0, j][0:1] for j in range(NJ)], 1)
        rhi_s[1, pl.ds(z, 1), :] = jnp.concatenate([t[NI - 1, j][S - 1:S] for j in range(NJ)], 1)
        return pack_cols(z, [t[i, 0] for i in range(NI)], [t[i, NJ - 1] for i in range(NI)], acc)

    store_cols(1, lax.fori_loop(0, ZF, k_layer, zeros()))
    loads[2].wait()

    def g_layer(z, acc):
        rlo_s[0, pl.ds(z, 1), :] = floor0[z, 0:1, :]
        rhi_s[0, pl.ds(z, 1), :] = floor0[z, CX - 1:CX, :]
        return pack_cols(z, [tile(floor0, z, i, 0) for i in range(NI)],
                         [tile(floor0, z, i, NJ - 1) for i in range(NI)], acc)

    store_cols(0, lax.fori_loop(0, ZF, g_layer, zeros()))
    start_if(f0)

    def floor_layer(first, src, dst, z, top, bottom):
        g, kxt, kyt = {}, {}, {}
        span = [(i, j) for i in range(NI) for j in range(NJ)]
        for i, j in span:
            g[i, j] = tile(src, z, i, j)
        if first:
            k = {ij: tile(kh, z, *ij) for ij in span}
            for i, j in span:
                r = pltpu.roll(k[i, j], S - 1, 0)
                if i < NI - 1:
                    v = k[i, j] + jnp.where(row_last, pltpu.roll(k[i + 1, j], S - 1, 0), r)
                else:
                    v = jnp.where(row_last, 0.0, k[i, j] + r)
                kxt[i, j] = v
                kx[z, pl.ds(i * S, S), pl.ds(j * L, L)] = v
                r = pltpu.roll(k[i, j], L - 1, 1)
                if j < NJ - 1:
                    v = k[i, j] + jnp.where(lane_last, pltpu.roll(k[i, j + 1], L - 1, 1), r)
                else:
                    v = jnp.where(lane_last, 0.0, k[i, j] + r)
                kyt[i, j] = v
                ky[z, pl.ds(i * S, S), pl.ds(j * L, L)] = v
                if bottom:
                    v = k[i, j]
                else:
                    v = k[i, j] + tile(kh, z + 1, i, j)
                kz[z, pl.ds(i * S, S), pl.ds(j * L, L)] = v
        else:
            for i, j in span:
                kxt[i, j] = tile(kx, z, i, j)
                kyt[i, j] = tile(ky, z, i, j)
        rx = {ij: pltpu.roll(g[ij], S - 1, 0) for ij in span}
        ry = {ij: pltpu.roll(g[ij], L - 1, 1) for ij in span}
        fx, fy, sx, sy = {}, {}, {}, {}
        for i, j in span:
            nx = rx[i, j] if i == NI - 1 else jnp.where(row_last, rx[i + 1, j], rx[i, j])
            ny = ry[i, j] if j == NJ - 1 else jnp.where(lane_last, ry[i, j + 1], ry[i, j])
            fx[i, j] = kxt[i, j] * (nx - g[i, j])
            fy[i, j] = kyt[i, j] * (ny - g[i, j])
            sx[i, j] = pltpu.roll(fx[i, j], 1, 0)
            sy[i, j] = pltpu.roll(fy[i, j], 1, 1)
        for i, j in span:
            px = jnp.where(row_first, sx[(i - 1) % NI, j], sx[i, j])
            py = jnp.where(lane_first, sy[i, (j - 1) % NJ], sy[i, j])
            if bottom:
                down = tile(kz, z, i, j) * g[i, j]
                new = g[i, j] - down
            else:
                new = g[i, j] + tile(kz, z, i, j) * (tile(src, z + 1, i, j) - g[i, j])
            if not top:
                new = new - tile(kz, z - 1, i, j) * (g[i, j] - tile(src, z - 1, i, j))
            new = new + ((fx[i, j] - px) + (fy[i, j] - py))
            dst[z, pl.ds(i * S, S), pl.ds(j * L, L)] = new

    def floor_sweep(first, src, dst):
        floor_layer(first, src, dst, 0, True, False)

        def body(z, carry):
            floor_layer(first, src, dst, z, False, False)
            return carry

        lax.fori_loop(1, ZF - 1, body, 0)
        floor_layer(first, src, dst, ZF - 1, False, True)

    def floor_edges(e, src, dst):
        g = 2 * e
        slot = 0 if e == 0 else 2
        rlo[slot] = (rlo_s[1] + rlo[1]) * (rlo[slot] - rlo_s[slot])
        rhi[slot] = (rhi_s[1] + rhi[1]) * (rhi[slot] - rhi_s[slot])
        clo[slot] = (clo_s[1] + clo[1]) * (clo[slot] - clo_s[slot])
        chi[slot] = (chi_s[1] + chi[1]) * (chi[slot] - chi_s[slot])
        dst[0] = dst[0] + HR * (bb[e] - src[0])

        def body(z, acc):
            row_lo, row_hi = rlo[slot, pl.ds(z, 1), :], rhi[slot, pl.ds(z, 1), :]
            t = {(i, j): tile(dst, z, i, j) for i in range(NI) for j in range(NJ)}
            for j in range(NJ):
                t[0, j] = t[0, j] + jnp.where(row_first, row_lo[:, j * L:j * L + L], 0.0)
                t[NI - 1, j] = t[NI - 1, j] + jnp.where(
                    row_last, row_hi[:, j * L:j * L + L], 0.0)
            for i in range(NI):
                low = pltpu.roll(clo[slot, pl.ds(i * S, S), :], lax.rem(L - z, L), 1)
                high = pltpu.roll(chi[slot, pl.ds(i * S, S), :], L - 1 - z, 1)
                t[i, 0] = t[i, 0] + jnp.where(lane_first, low, 0.0)
                t[i, NJ - 1] = t[i, NJ - 1] + jnp.where(lane_last, high, 0.0)
            for (i, j), v in t.items():
                dst[z, pl.ds(i * S, S), pl.ds(j * L, L)] = v
            if e == 1:
                return acc
            rlo_s[2, pl.ds(z, 1), :] = jnp.concatenate([t[0, j][0:1] for j in range(NJ)], 1)
            rhi_s[2, pl.ds(z, 1), :] = jnp.concatenate([t[NI - 1, j][S - 1:S] for j in range(NJ)], 1)
            return pack_cols(z, [t[i, 0] for i in range(NI)],
                             [t[i, NJ - 1] for i in range(NI)], acc)

        if e == 0:
            store_cols(2, lax.fori_loop(0, ZF, body, zeros()))
        else:
            lax.fori_loop(0, ZF, body, 0)

    NH, NK = R // S, NYW // L

    def tin_layer(e, src, dst, z, zu, zd, top):
        span = [(h, k) for h in range(NH) for k in range(NK)]
        s_x, s_y = speeds[0, z], speeds[1, z]
        keep = (1.0 - 6.0 * KT) - s_x - s_y
        u = {hk: tile(src, z, *hk) for hk in span}
        rd = {hk: pltpu.roll(u[hk], 1, 0) for hk in span}
        ru = {hk: pltpu.roll(u[hk], S - 1, 0) for hk in span}
        ld = {hk: pltpu.roll(u[hk], 1, 1) for hk in span}
        lu = {hk: pltpu.roll(u[hk], L - 1, 1) for hk in span}
        first_row, last_row = [], []
        before, after = tlo[e, pl.ds(z, 1), :], thi[e, pl.ds(z, 1), :]
        for h, k in span:
            v = u[h, k]
            below = before[:, k * L:k * L + L] if h == 0 else rd[h - 1, k]
            above = after[:, k * L:k * L + L] if h == NH - 1 else ru[h + 1, k]
            xm = jnp.where(row_first, below, rd[h, k])
            xp = jnp.where(row_last, above, ru[h, k])
            ym = jnp.where(lane_first, 0.0 if k == 0 else ld[h, k - 1], ld[h, k])
            yp = jnp.where(lane_last, 0.0 if k == NK - 1 else lu[h, k + 1], lu[h, k])
            f = tile(flow, z, h, k)
            total = ((xm + xp) + (ym + yp)) + (tile(src, zu, h, k) + tile(src, zd, h, k))
            new = keep * v + KT * total
            new = new + s_x * jnp.where((f & 1) == 0, xm, xp)
            new = new + s_y * jnp.where(f < 2, ym, yp)
            if top:
                new = new + HT * (pp[e, pl.ds(h * S, S), pl.ds(k * L, L)] - v)
            dst[z, pl.ds(h * S, S), pl.ds(k * L, L)] = new
            if h == 0:
                first_row.append(new[0:1])
            if h == NH - 1:
                last_row.append(new[S - 1:S])
        if e == 0:
            tlo_s[1, pl.ds(z, 1), :] = jnp.concatenate(first_row, 1)
            thi_s[1, pl.ds(z, 1), :] = jnp.concatenate(last_row, 1)

    def tin_sweep(e, src, dst):
        tin_layer(e, src, dst, 0, 1, 0, True)

        def body(z, carry):
            tin_layer(e, src, dst, z, jnp.minimum(z + 1, Z - 1), z - 1, False)
            return carry

        lax.fori_loop(1, Z, body, 0)

    floor_sweep(True, floor0, floor1)
    wait_recv_if(f0)
    for m in b0:
        m.wait_recv()
    own_b.wait()
    wait_send_if(f0)
    floor_edges(0, floor0, floor1)
    f1, p1 = floor_msgs(1), p_msgs(1, floor1)
    start_if(f1)
    for m in p1:
        m.start()
    own_p1 = pltpu.make_async_copy(
        floor1.at[0, pl.ds(pl.multiple_of(c * R, R), R), :],
        pp.at[1, :, pl.ds(pl.multiple_of(c * CY, CY), CY)], load_sem.at[6])
    own_p1.start()

    loads[3].wait()
    wait_recv_if(t0)
    for m in p0:
        m.wait_recv()
    own_p.wait()
    tin_sweep(0, tin0, tin1)
    t1, b1 = tin_msgs(1), b_msgs(1, tin1)
    start_if(t1)
    for m in b1:
        m.start()
    own_b1 = pltpu.make_async_copy(
        tin1.at[0, :, pl.ds(pl.multiple_of(c * CY, CY), CY)],
        bb.at[1, pl.ds(pl.multiple_of(c * R, R), R), :], load_sem.at[7])
    own_b1.start()

    floor_sweep(False, floor1, floor_o)
    wait_recv_if(f1)
    for m in b1:
        m.wait_recv()
    own_b1.wait()
    wait_send_if(f1)
    floor_edges(1, floor1, floor_o)

    wait_recv_if(t1)
    for m in p1:
        m.wait_recv()
    own_p1.wait()
    tin_sweep(1, tin1, tin_o)

    wait_send_if(t0)
    wait_send_if(t1)
    for m in p0 + b0 + p1 + b1:
        m.wait_send()


def local(n, ty, tin_temp, flow_code, speeds, floor_temp, material, conductivity):
    tin_shape = tin_temp.shape
    floor_shape = floor_temp.shape[1:]
    Z, R, NYW = tin_shape
    ZF, CX, CY = floor_shape
    f32, i32 = jnp.float32, jnp.int32
    V = pltpu.VMEM
    tin_v, floor_v = V(tin_shape, f32), V(floor_shape, f32)
    edge_t = V((2, Z, NYW), f32)
    edge_r = V((3, ZF, CY), f32)
    edge_c = V((3, CX, L), f32)
    tin_out, floor_out = pl.pallas_call(
        functools.partial(kernel, n, ty),
        out_shape=OUT(tin_shape, floor_shape),
        in_specs=[pl.BlockSpec(memory_space=m) for m in
                  (pl.ANY, pl.ANY, pltpu.SMEM, pl.ANY, pl.ANY, pltpu.SMEM)],
        out_specs=[pl.BlockSpec(memory_space=pltpu.VMEM)] * 2,
        scratch_shapes=[
            tin_v, V(tin_shape, i32), tin_v, floor_v, V(floor_shape, i32), floor_v,
            floor_v, floor_v, floor_v, floor_v,
            edge_t, edge_t, edge_t, edge_t,
            edge_r, edge_r, edge_r, edge_r,
            edge_c, edge_c, edge_c, edge_c,
            V((2, R, NYW), f32), V((2, CX, CY), f32),
            pltpu.SemaphoreType.DMA((8,)),
            pltpu.SemaphoreType.DMA((2, 12)),
            pltpu.SemaphoreType.DMA((2, 12)),
        ],
        compiler_params=pltpu.CompilerParams(
            collective_id=0, has_side_effects=True, vmem_limit_bytes=52 * 1024 * 1024),
        cost_estimate=pl.CostEstimate(flops=120_000_000, bytes_accessed=23_000_000, transcendentals=0),
    )(tin_temp, flow_code, speeds, floor_temp[0], material[0], conductivity)
    return tin_out, floor_out[None]


def OUT(tin_shape, floor_shape):
    return [jax.ShapeDtypeStruct(tin_shape, jnp.float32),
            jax.ShapeDtypeStruct(floor_shape, jnp.float32)]


def solution(mesh):
    n = mesh.shape["len"]
    split = ("grp", "len")
    placed = (P(None, split, None), P(None, split, None), P(),
              P(split, None, None, None), P(split, None, None, None), P())

    def whole(tin_temp, flow_code, speeds, floor_temp, material, conductivity):
        ty = tin_temp.shape[2] // floor_temp.shape[3]
        return jax.shard_map(
            functools.partial(local, n, ty),
            mesh=mesh,
            in_specs=placed,
            out_specs=(P(None, split, None), P(split, None, None, None)),
            check_vma=False,
        )(tin_temp, flow_code, speeds, floor_temp, material, conductivity)

    return whole
```

profile of v0, /device:TPU:0, one launch (start us, length us, event | category | flops | bytes accessed | tf_op | source)
XLA Modules:
  0.0 67.4 jit_solution(12081107843488346898)
XLA Ops:
  0.6 0.0 copy-start
  0.6 0.7 copy-done
  1.3 0.0 copy-start.1
  1.3 0.7 copy-done.1
  2.0 58.8 %shard_map.77 = (f32[64,16,1024]{2,1,0:T(8,128)}, f32[48,64,256]{2,1,0:T(8,128)}) custom-call(f32[64,16,1024]{2,1,0:T(8,128)} %tin_h.1, s32[64,16,1024]{2,1,0:T(8,128)} %flow_h.1, f32[2,64]{1,0:T(2,128)S(1)} %copy-done, f32[48,64,256]{2,1,0:T(8,128)} %bitcast.4, s32[48,64,256]{2,1,0:T(8,128)} %bitcast.5, f32[3]{0:T(128)S(1)} %copy-done.1), custom_call_target="tpu_custom_call" | custom-call | flops 120000000 | bytes 23000000 | tf_op jit(solution)/shard_map/pallas_call | solution.py:406
  60.7 0.0 copy-start.2
  60.8 4.9 %copy.10 = f32[64,16,1024]{2,1,0:T(8,128)} copy(f32[64,16,1024]{2,1,0:T(8,128)} %get-tuple-element.8) | data formatting | bytes 8388608
  65.7 0.0 copy-done.2
  65.7 1.7 %copy.11 = f32[1,48,64,256]{3,2,1,0:T(8,128)} copy(f32[1,48,64,256]{3,2,1,0:T(8,128)S(1)} %bitcast.3) | data formatting | bytes 6291456
Async XLA Ops:
  0.6 0.7 %copy-start = (f32[2,64]{1,0:T(2,128)S(1)}, f32[2,64]{1,0:T(2,128)}, u32[]{:S(2)}) copy-start(f32[2,64]{1,0:T(2,128)} %speeds.1) | copy-start | bytes 1540
  1.3 0.7 copy-start.1
  60.7 5.0 %copy-start.2 = (f32[48,64,256]{2,1,0:T(8,128)S(1)}, f32[48,64,256]{2,1,0:T(8,128)}, u32[]{:S(2)}) copy-start(f32[48,64,256]{2,1,0:T(8,128)} %get-tuple-element.5) | copy-start | bytes 9437188
where the time goes:
time: 68.3 us; the launch traced here: 67.4 us
  Pallas kernels  58.8 us (86%)
  local copies, waits for them, and re-layouts  7.93 us (12%)
    pallas_call x1, Pallas kernels, local(): pl.pallas_call(functools.partial(kernel, n, ty), out_shape=OUT(tin_shape,...  58.8 us
    unnamed x8, local copies, waits for them, and re-layouts  7.93 us

commit v1 on v0

--- a/solution.py
+++ b/solution.py
@@ -11,12 +11,13 @@
 HT = 0.2
 HR = 0.2
 L = 128
+NQ = 4
 S = 8
 
 
-def kernel(n, ty, tin_h, flow_h, speeds, floor_h, mat_h, cond,
+def kernel(n, ty, tin_h, flow_h, speeds_h, floor_h, mat_h, cond_h,
            tin_o, floor_o,
-           tin0, flow, tin1, floor0, mat, floor1, kh, kx, ky, kz,
+           speeds, cond, tin0, flow, tin1, floor0, mat, floor1, kh, kx, ky, kz,
            tlo, thi, tlo_s, thi_s,
            rlo, rhi, rlo_s, rhi_s,
            clo, chi, clo_s, chi_s,
@@ -32,6 +33,10 @@
 
     loads = [pltpu.make_async_copy(a, b, load_sem.at[i]) for i, (a, b) in enumerate(
         [(tin_h, tin0), (mat_h, mat), (floor_h, floor0), (flow_h, flow)])]
+    scalars = [pltpu.make_async_copy(cond_h, cond, load_sem.at[8]),
+               pltpu.make_async_copy(speeds_h, speeds, load_sem.at[9])]
+    for ld in scalars:
+        ld.start()
     for ld in loads:
         ld.start()
 
@@ -71,9 +76,12 @@
             recv_sem=recv_sem.at[e, slot], device_id={"len": target},
             device_id_type=pl.DeviceIdType.MESH)
 
-    def tin_msgs(e):
-        return [(up_ok, dn_ok, remote(e, 0, thi_s.at[e], tlo.at[e], me + 1), tlo),
-                (dn_ok, up_ok, remote(e, 1, tlo_s.at[e], thi.at[e], me - 1), thi)]
+    ZQ = Z // NQ
+
+    def tin_msgs(e, q):
+        part = pl.ds(q * ZQ, ZQ)
+        return [(up_ok, dn_ok, remote(e, 12 + q, thi_s.at[e, part], tlo.at[e, part], me + 1), tlo),
+                (dn_ok, up_ok, remote(e, 12 + NQ + q, tlo_s.at[e, part], thi.at[e, part], me - 1), thi)]
 
     def floor_msgs(e):
         if e == 0:
@@ -127,7 +135,7 @@
     def tile(ref, z, i, j):
         return ref[z, pl.ds(i * S, S), pl.ds(j * L, L)]
 
-    for _, ok, _, buf in tin_msgs(0) + floor_msgs(0):
+    for _, ok, _, buf in tin_msgs(0, 0) + floor_msgs(0):
         @pl.when(jnp.logical_not(ok))
         def _():
             buf[...] = jnp.zeros_like(buf)
@@ -146,13 +154,16 @@
         peers = peers + ok.astype(jnp.int32)
     pl.semaphore_wait(barrier, peers)
 
-    t0, f0 = tin_msgs(0), floor_msgs(0)
+    t0, f0 = [tin_msgs(0, q) for q in range(NQ)], floor_msgs(0)
+    t1 = [tin_msgs(1, q) for q in range(NQ)]
     p0, b0 = p_msgs(0, floor_h), b_msgs(0, tin_h)
-    start_if(t0)
-    for m in b0 + p0:
+    for m in p0 + b0:
         m.start()
+    for q in range(NQ):
+        start_if(t0[q])
 
     loads[1].wait()
+    scalars[0].wait()
     c0, c1, c2 = cond[0] * 0.5, cond[1] * 0.5, cond[2] * 0.5
     NI, NJ = CX // S, CY // L
 
@@ -184,7 +195,7 @@
         rhi_s[1, pl.ds(z, 1), :] = jnp.concatenate([t[NI - 1, j][S - 1:S] for j in range(NJ)], 1)
         return pack_cols(z, [t[i, 0] for i in range(NI)], [t[i, NJ - 1] for i in range(NI)], acc)
 
-    store_cols(1, lax.fori_loop(0, ZF, k_layer, zeros()))
+    store_cols(1, lax.fori_loop(0, ZF, k_layer, zeros(), unroll=4))
     loads[2].wait()
 
     def g_layer(z, acc):
@@ -193,7 +204,7 @@
         return pack_cols(z, [tile(floor0, z, i, 0) for i in range(NI)],
                          [tile(floor0, z, i, NJ - 1) for i in range(NI)], acc)
 
-    store_cols(0, lax.fori_loop(0, ZF, g_layer, zeros()))
+    store_cols(0, lax.fori_loop(0, ZF, g_layer, zeros(), unroll=4))
     start_if(f0)
 
     def floor_layer(first, src, dst, z, top, bottom):
@@ -291,9 +302,9 @@
                              [t[i, NJ - 1] for i in range(NI)], acc)
 
         if e == 0:
-            store_cols(2, lax.fori_loop(0, ZF, body, zeros()))
+            store_cols(2, lax.fori_loop(0, ZF, body, zeros(), unroll=4))
         else:
-            lax.fori_loop(0, ZF, body, 0)
+            lax.fori_loop(0, ZF, body, 0, unroll=4)
 
     NH, NK = R // S, NYW // L
 
@@ -332,16 +343,36 @@
             tlo_s[1, pl.ds(z, 1), :] = jnp.concatenate(first_row, 1)
             thi_s[1, pl.ds(z, 1), :] = jnp.concatenate(last_row, 1)
 
-    def tin_sweep(e, src, dst):
-        tin_layer(e, src, dst, 0, 1, 0, True)
+    def tin_sweep(e, src, dst, q):
+        if q == 0:
+            tin_layer(e, src, dst, 0, 1, 0, True)
 
         def body(z, carry):
             tin_layer(e, src, dst, z, jnp.minimum(z + 1, Z - 1), z - 1, False)
             return carry
 
-        lax.fori_loop(1, Z, body, 0)
+        lax.fori_loop(max(1, q * ZQ), (q + 1) * ZQ, body, 0)
 
     floor_sweep(True, floor0, floor1)
+
+    loads[3].wait()
+    scalars[1].wait()
+    for m in p0:
+        m.wait_recv()
+    own_p.wait()
+    b1 = b_msgs(1, tin1)
+    own_b1 = pltpu.make_async_copy(
+        tin1.at[0, :, pl.ds(pl.multiple_of(c * CY, CY), CY)],
+        bb.at[1, pl.ds(pl.multiple_of(c * R, R), R), :], load_sem.at[7])
+    for q in range(NQ):
+        wait_recv_if(t0[q])
+        tin_sweep(0, tin0, tin1, q)
+        start_if(t1[q])
+        if q == 0:
+            for m in b1:
+                m.start()
+            own_b1.start()
+
     wait_recv_if(f0)
     for m in b0:
         m.wait_recv()
@@ -349,30 +380,22 @@
     wait_send_if(f0)
     floor_edges(0, floor0, floor1)
     f1, p1 = floor_msgs(1), p_msgs(1, floor1)
-    start_if(f1)
     for m in p1:
         m.start()
+    start_if(f1)
     own_p1 = pltpu.make_async_copy(
         floor1.at[0, pl.ds(pl.multiple_of(c * R, R), R), :],
         pp.at[1, :, pl.ds(pl.multiple_of(c * CY, CY), CY)], load_sem.at[6])
     own_p1.start()
 
-    loads[3].wait()
-    wait_recv_if(t0)
-    for m in p0:
+    floor_sweep(False, floor1, floor_o)
+    for m in p1:
         m.wait_recv()
-    own_p.wait()
-    tin_sweep(0, tin0, tin1)
-    t1, b1 = tin_msgs(1), b_msgs(1, tin1)
-    start_if(t1)
-    for m in b1:
-        m.start()
-    own_b1 = pltpu.make_async_copy(
-        tin1.at[0, :, pl.ds(pl.multiple_of(c * CY, CY), CY)],
-        bb.at[1, pl.ds(pl.multiple_of(c * R, R), R), :], load_sem.at[7])
-    own_b1.start()
-
-    floor_sweep(False, floor1, floor_o)
+    own_p1.wait()
+    for q in range(NQ):
+        wait_recv_if(t1[q])
+        tin_sweep(1, tin1, tin_o, q)
+
     wait_recv_if(f1)
     for m in b1:
         m.wait_recv()
@@ -380,14 +403,9 @@
     wait_send_if(f1)
     floor_edges(1, floor1, floor_o)
 
-    wait_recv_if(t1)
-    for m in p1:
-        m.wait_recv()
-    own_p1.wait()
-    tin_sweep(1, tin1, tin_o)
-
-    wait_send_if(t0)
-    wait_send_if(t1)
+    for q in range(NQ):
+        wait_send_if(t0[q])
+        wait_send_if(t1[q])
     for m in p0 + b0 + p1 + b1:
         m.wait_send()
 
@@ -407,29 +425,29 @@
         functools.partial(kernel, n, ty),
         out_shape=OUT(tin_shape, floor_shape),
         in_specs=[pl.BlockSpec(memory_space=m) for m in
-                  (pl.ANY, pl.ANY, pltpu.SMEM, pl.ANY, pl.ANY, pltpu.SMEM)],
+                  (pltpu.HBM,) * 6],
         out_specs=[pl.BlockSpec(memory_space=pltpu.VMEM)] * 2,
         scratch_shapes=[
+            pltpu.SMEM(speeds.shape, f32), pltpu.SMEM(conductivity.shape, f32),
             tin_v, V(tin_shape, i32), tin_v, floor_v, V(floor_shape, i32), floor_v,
             floor_v, floor_v, floor_v, floor_v,
             edge_t, edge_t, edge_t, edge_t,
             edge_r, edge_r, edge_r, edge_r,
             edge_c, edge_c, edge_c, edge_c,
             V((2, R, NYW), f32), V((2, CX, CY), f32),
-            pltpu.SemaphoreType.DMA((8,)),
-            pltpu.SemaphoreType.DMA((2, 12)),
-            pltpu.SemaphoreType.DMA((2, 12)),
+            pltpu.SemaphoreType.DMA((10,)),
+            pltpu.SemaphoreType.DMA((2, 12 + 2 * NQ)),
+            pltpu.SemaphoreType.DMA((2, 12 + 2 * NQ)),
         ],
         compiler_params=pltpu.CompilerParams(
-            collective_id=0, has_side_effects=True, vmem_limit_bytes=52 * 1024 * 1024),
+            collective_id=0, has_side_effects=True, vmem_limit_bytes=44 * 1024 * 1024),
         cost_estimate=pl.CostEstimate(flops=120_000_000, bytes_accessed=23_000_000, transcendentals=0),
     )(tin_temp, flow_code, speeds, floor_temp[0], material[0], conductivity)
     return tin_out, floor_out[None]
 
 
 def OUT(tin_shape, floor_shape):
-    return [jax.ShapeDtypeStruct(tin_shape, jnp.float32),
-            jax.ShapeDtypeStruct(floor_shape, jnp.float32)]
+    return [pltpu.VMEM(tin_shape, jnp.float32), pltpu.VMEM(floor_shape, jnp.float32)]
 
 
 def solution(mesh):

time: 68.3 us -> 49.7 us (0.73); the launches traced: 67.4 us -> 49.5 us
  Pallas kernels: 58.8 us -> 43.8 us
  local copies, waits for them, and re-layouts: 7.93 us -> 5.01 us
    pallas_call x1, Pallas kernels: 58.8 us -> 43.8 us  [local(): pl.pallas_call(functools.partial(kernel, n, ty), out_shape=OUT(tin_shape,...]
    unnamed x8 -> x6, local copies, waits for them, and re-layouts: 7.93 us -> 5.01 us
where the time goes in v1:
time: 49.7 us; the launch traced here: 49.5 us
  Pallas kernels  43.8 us (88%)
  local copies, waits for them, and re-layouts  5.01 us (10%)
  between operations  0.65 us (1%)
    pallas_call x1, Pallas kernels, local(): pl.pallas_call(functools.partial(kernel, n, ty), out_shape=OUT(tin_shape,...  43.8 us
    unnamed x6, local copies, waits for them, and re-layouts  5.01 us

profile of v1, /device:TPU:0, one launch (start us, length us, event | category | flops | bytes accessed | tf_op | source)
XLA Modules:
  0.0 49.5 jit_solution(17878800794497955405)
XLA Ops:
  0.6 0.0 copy-start
  0.6 0.7 %copy-done = f32[2,64]{1,0:T(2,128)S(1)} copy-done((f32[2,64]{1,0:T(2,128)S(1)}, f32[2,64]{1,0:T(2,128)}, u32[]{:S(2)}) %copy-start) | copy-done | bytes 536
  1.3 0.0 copy-start.1
  1.3 0.7 %copy-done.1 = f32[3]{0:T(128)S(1)} copy-done((f32[3]{0:T(128)S(1)}, f32[3]{0:T(128)}, u32[]{:S(2)}) %copy-start.1) | copy-done | bytes 36
  2.0 43.8 %shard_map.77 = (f32[64,16,1024]{2,1,0:T(8,128)S(1)}, f32[48,64,256]{2,1,0:T(8,128)S(1)}) custom-call(f32[64,16,1024]{2,1,0:T(8,128)} %tin_h.1, s32[64,16,1024]{2,1,0:T(8,128)} %flow_h.1, f32[2,64]{1,0:T(2,128)S(1)} %copy-done, f32[48,64,256]{2,1,0:T(8,128)} %bitcast.4, s32[48,64,256]{2,1,0:T(8,128)} %bitcast.5, f32[3]{0:T(128)S(1)} %copy-done.1), custom_call_target="tpu_custom_call" | custom-call | flops 120000000 | bytes 23000000 | tf_op jit(solution)/shard_map/pallas_call | solution.py:424
  45.8 2.0 %copy.10 = f32[64,16,1024]{2,1,0:T(8,128)} copy(f32[64,16,1024]{2,1,0:T(8,128)S(1)} %get-tuple-element.6) | data formatting | bytes 8388608
  47.8 1.7 %copy.11 = f32[1,48,64,256]{3,2,1,0:T(8,128)} copy(f32[1,48,64,256]{3,2,1,0:T(8,128)S(1)} %bitcast.3) | data formatting | bytes 6291456
Async XLA Ops:
  0.6 0.7 %copy-start = (f32[2,64]{1,0:T(2,128)S(1)}, f32[2,64]{1,0:T(2,128)}, u32[]{:S(2)}) copy-start(f32[2,64]{1,0:T(2,128)} %speeds_h.1) | copy-start | bytes 1540
  1.3 0.7 %copy-start.1 = (f32[3]{0:T(128)S(1)}, f32[3]{0:T(128)}, u32[]{:S(2)}) copy-start(f32[3]{0:T(128)} %cond_h.1) | copy-start | bytes 40

commit v2 on v1

--- a/solution.py
+++ b/solution.py
@@ -12,6 +12,8 @@
 HR = 0.2
 L = 128
 NQ = 4
+TU = 4
+FU = 2
 S = 8
 
 
@@ -208,58 +210,64 @@
     start_if(f0)
 
     def floor_layer(first, src, dst, z, top, bottom):
-        g, kxt, kyt = {}, {}, {}
-        span = [(i, j) for i in range(NI) for j in range(NJ)]
-        for i, j in span:
-            g[i, j] = tile(src, z, i, j)
+        def put(ref, i, j, v):
+            ref[z, pl.ds(i * S, S), pl.ds(j * L, L)] = v
+            return v
+
+        def next_x(roll, i, j):
+            if i == NI - 1:
+                return roll(i, j)
+            return jnp.where(row_last, roll(i + 1, j), roll(i, j))
+
+        def next_y(roll, i, j):
+            if j == NJ - 1:
+                return roll(i, j)
+            return jnp.where(lane_last, roll(i, j + 1), roll(i, j))
+
+        def rolled(get, amount, dim):
+            return functools.cache(lambda i, j: pltpu.roll(get(i, j), amount, dim))
+
+        g = functools.cache(lambda i, j: tile(src, z, i, j))
+        gx, gy = rolled(g, S - 1, 0), rolled(g, L - 1, 1)
         if first:
-            k = {ij: tile(kh, z, *ij) for ij in span}
-            for i, j in span:
-                r = pltpu.roll(k[i, j], S - 1, 0)
-                if i < NI - 1:
-                    v = k[i, j] + jnp.where(row_last, pltpu.roll(k[i + 1, j], S - 1, 0), r)
+            k = functools.cache(lambda i, j: tile(kh, z, i, j))
+            k_x, k_y = rolled(k, S - 1, 0), rolled(k, L - 1, 1)
+
+            def face_x(i, j):
+                v = k(i, j) + next_x(k_x, i, j)
+                return put(kx, i, j, jnp.where(row_last, 0.0, v) if i == NI - 1 else v)
+
+            def face_y(i, j):
+                v = k(i, j) + next_y(k_y, i, j)
+                return put(ky, i, j, jnp.where(lane_last, 0.0, v) if j == NJ - 1 else v)
+
+            def face_z(i, j):
+                return put(kz, i, j, k(i, j) if bottom else k(i, j) + tile(kh, z + 1, i, j))
+        else:
+            def face_x(i, j):
+                return tile(kx, z, i, j)
+
+            def face_y(i, j):
+                return tile(ky, z, i, j)
+
+            def face_z(i, j):
+                return tile(kz, z, i, j)
+
+        fx = functools.cache(lambda i, j: face_x(i, j) * (next_x(gx, i, j) - g(i, j)))
+        fy = functools.cache(lambda i, j: face_y(i, j) * (next_y(gy, i, j) - g(i, j)))
+        sx, sy = rolled(fx, 1, 0), rolled(fy, 1, 1)
+        for i in range(NI):
+            for j in range(NJ):
+                px = jnp.where(row_first, sx(i - 1, j) if i else 0.0, sx(i, j))
+                py = jnp.where(lane_first, sy(i, j - 1) if j else 0.0, sy(i, j))
+                v = g(i, j)
+                if bottom:
+                    new = v - face_z(i, j) * v
                 else:
-                    v = jnp.where(row_last, 0.0, k[i, j] + r)
-                kxt[i, j] = v
-                kx[z, pl.ds(i * S, S), pl.ds(j * L, L)] = v
-                r = pltpu.roll(k[i, j], L - 1, 1)
-                if j < NJ - 1:
-                    v = k[i, j] + jnp.where(lane_last, pltpu.roll(k[i, j + 1], L - 1, 1), r)
-                else:
-                    v = jnp.where(lane_last, 0.0, k[i, j] + r)
-                kyt[i, j] = v
-                ky[z, pl.ds(i * S, S), pl.ds(j * L, L)] = v
-                if bottom:
-                    v = k[i, j]
-                else:
-                    v = k[i, j] + tile(kh, z + 1, i, j)
-                kz[z, pl.ds(i * S, S), pl.ds(j * L, L)] = v
-        else:
-            for i, j in span:
-                kxt[i, j] = tile(kx, z, i, j)
-                kyt[i, j] = tile(ky, z, i, j)
-        rx = {ij: pltpu.roll(g[ij], S - 1, 0) for ij in span}
-        ry = {ij: pltpu.roll(g[ij], L - 1, 1) for ij in span}
-        fx, fy, sx, sy = {}, {}, {}, {}
-        for i, j in span:
-            nx = rx[i, j] if i == NI - 1 else jnp.where(row_last, rx[i + 1, j], rx[i, j])
-            ny = ry[i, j] if j == NJ - 1 else jnp.where(lane_last, ry[i, j + 1], ry[i, j])
-            fx[i, j] = kxt[i, j] * (nx - g[i, j])
-            fy[i, j] = kyt[i, j] * (ny - g[i, j])
-            sx[i, j] = pltpu.roll(fx[i, j], 1, 0)
-            sy[i, j] = pltpu.roll(fy[i, j], 1, 1)
-        for i, j in span:
-            px = jnp.where(row_first, sx[(i - 1) % NI, j], sx[i, j])
-            py = jnp.where(lane_first, sy[i, (j - 1) % NJ], sy[i, j])
-            if bottom:
-                down = tile(kz, z, i, j) * g[i, j]
-                new = g[i, j] - down
-            else:
-                new = g[i, j] + tile(kz, z, i, j) * (tile(src, z + 1, i, j) - g[i, j])
-            if not top:
-                new = new - tile(kz, z - 1, i, j) * (g[i, j] - tile(src, z - 1, i, j))
-            new = new + ((fx[i, j] - px) + (fy[i, j] - py))
-            dst[z, pl.ds(i * S, S), pl.ds(j * L, L)] = new
+                    new = v + face_z(i, j) * (tile(src, z + 1, i, j) - v)
+                if not top:
+                    new = new - tile(kz, z - 1, i, j) * (v - tile(src, z - 1, i, j))
+                put(dst, i, j, new + ((fx(i, j) - px) + (fy(i, j) - py)))
 
     def floor_sweep(first, src, dst):
         floor_layer(first, src, dst, 0, True, False)
@@ -268,7 +276,7 @@
             floor_layer(first, src, dst, z, False, False)
             return carry
 
-        lax.fori_loop(1, ZF - 1, body, 0)
+        lax.fori_loop(1, ZF - 1, body, 0, unroll=FU)
         floor_layer(first, src, dst, ZF - 1, False, True)
 
     def floor_edges(e, src, dst):
@@ -309,24 +317,24 @@
     NH, NK = R // S, NYW // L
 
     def tin_layer(e, src, dst, z, zu, zd, top):
-        span = [(h, k) for h in range(NH) for k in range(NK)]
         s_x, s_y = speeds[0, z], speeds[1, z]
         keep = (1.0 - 6.0 * KT) - s_x - s_y
-        u = {hk: tile(src, z, *hk) for hk in span}
-        rd = {hk: pltpu.roll(u[hk], 1, 0) for hk in span}
-        ru = {hk: pltpu.roll(u[hk], S - 1, 0) for hk in span}
-        ld = {hk: pltpu.roll(u[hk], 1, 1) for hk in span}
-        lu = {hk: pltpu.roll(u[hk], L - 1, 1) for hk in span}
         first_row, last_row = [], []
         before, after = tlo[e, pl.ds(z, 1), :], thi[e, pl.ds(z, 1), :]
+        u = functools.cache(lambda h, k: tile(src, z, h, k))
+        rd = functools.cache(lambda h, k: pltpu.roll(u(h, k), 1, 0))
+        ru = functools.cache(lambda h, k: pltpu.roll(u(h, k), S - 1, 0))
+        ld = functools.cache(lambda h, k: pltpu.roll(u(h, k), 1, 1))
+        lu = functools.cache(lambda h, k: pltpu.roll(u(h, k), L - 1, 1))
+        span = [(h, k) for k in range(NK) for h in range(NH)]
         for h, k in span:
-            v = u[h, k]
-            below = before[:, k * L:k * L + L] if h == 0 else rd[h - 1, k]
-            above = after[:, k * L:k * L + L] if h == NH - 1 else ru[h + 1, k]
-            xm = jnp.where(row_first, below, rd[h, k])
-            xp = jnp.where(row_last, above, ru[h, k])
-            ym = jnp.where(lane_first, 0.0 if k == 0 else ld[h, k - 1], ld[h, k])
-            yp = jnp.where(lane_last, 0.0 if k == NK - 1 else lu[h, k + 1], lu[h, k])
+            v = u(h, k)
+            below = before[:, k * L:k * L + L] if h == 0 else rd(h - 1, k)
+            above = after[:, k * L:k * L + L] if h == NH - 1 else ru(h + 1, k)
+            xm = jnp.where(row_first, below, rd(h, k))
+            xp = jnp.where(row_last, above, ru(h, k))
+            ym = jnp.where(lane_first, 0.0 if k == 0 else ld(h, k - 1), ld(h, k))
+            yp = jnp.where(lane_last, 0.0 if k == NK - 1 else lu(h, k + 1), lu(h, k))
             f = tile(flow, z, h, k)
             total = ((xm + xp) + (ym + yp)) + (tile(src, zu, h, k) + tile(src, zd, h, k))
             new = keep * v + KT * total
@@ -351,7 +359,7 @@
             tin_layer(e, src, dst, z, jnp.minimum(z + 1, Z - 1), z - 1, False)
             return carry
 
-        lax.fori_loop(max(1, q * ZQ), (q + 1) * ZQ, body, 0)
+        lax.fori_loop(max(1, q * ZQ), (q + 1) * ZQ, body, 0, unroll=TU)
 
     floor_sweep(True, floor0, floor1)
 
@@ -442,7 +450,8 @@
         compiler_params=pltpu.CompilerParams(
             collective_id=0, has_side_effects=True, vmem_limit_bytes=44 * 1024 * 1024),
         cost_estimate=pl.CostEstimate(flops=120_000_000, bytes_accessed=23_000_000, transcendentals=0),
-    )(tin_temp, flow_code, speeds, floor_temp[0], material[0], conductivity)
+    )(tin_temp, flow_code, pltpu.with_memory_space_constraint(speeds, pltpu.HBM), floor_temp[0],
+      material[0], pltpu.with_memory_space_constraint(conductivity, pltpu.HBM))
     return tin_out, floor_out[None]
 
 

time: 49.7 us -> 35.5 us (0.71)
  Pallas kernels: 43.8 us -> 31.1 us
  local copies, waits for them, and re-layouts: 5.01 us -> 3.68 us
    pallas_call x1, Pallas kernels: 43.8 us -> 31.1 us  [local(): pl.pallas_call(functools.partial(kernel, n, ty), out_shape=OUT(tin_shape,...]
    unnamed x6 -> x2, local copies, waits for them, and re-layouts: 5.01 us -> 3.68 us
where the time goes in v2:
time: 35.5 us; the launch traced here: 35.4 us
  Pallas kernels  31.1 us (88%)
  local copies, waits for them, and re-layouts  3.68 us (10%)
  between operations  0.64 us (2%)
    pallas_call x1, Pallas kernels, local(): pl.pallas_call(functools.partial(kernel, n, ty), out_shape=OUT(tin_shape,...  31.1 us
    unnamed x2, local copies, waits for them, and re-layouts  3.68 us

profile of v2, /device:TPU:0, one launch (start us, length us, event | category | flops | bytes accessed | tf_op | source)
XLA Modules:
  0.0 35.4 jit_solution(263597769281386004)
XLA Ops:
  0.6 31.1 %shard_map.77 = (f32[64,16,1024]{2,1,0:T(8,128)S(1)}, f32[48,64,256]{2,1,0:T(8,128)S(1)}) custom-call(f32[64,16,1024]{2,1,0:T(8,128)} %tin_h.1, s32[64,16,1024]{2,1,0:T(8,128)} %flow_h.1, f32[2,64]{1,0:T(2,128)} %speeds_h.1, f32[48,64,256]{2,1,0:T(8,128)} %bitcast.4, s32[48,64,256]{2,1,0:T(8,128)} %bitcast.5, f32[3]{0:T(128)} %cond_h.1), custom_call_target="tpu_custom_call" | custom-call | flops 120000000 | bytes 23000000 | tf_op jit(solution)/shard_map/pallas_call | solution.py:432
  31.7 2.0 %copy.10 = f32[64,16,1024]{2,1,0:T(8,128)} copy(f32[64,16,1024]{2,1,0:T(8,128)S(1)} %get-tuple-element.6) | data formatting | bytes 8388608
  33.7 1.7 %copy.11 = f32[1,48,64,256]{3,2,1,0:T(8,128)} copy(f32[1,48,64,256]{3,2,1,0:T(8,128)S(1)} %bitcast.3) | data formatting | bytes 6291456

commit v3 on v2

--- a/solution.py
+++ b/solution.py
@@ -13,7 +13,7 @@
 L = 128
 NQ = 4
 TU = 4
-FU = 2
+FU = 3
 S = 8
 
 
@@ -149,7 +149,7 @@
         thi_s[0, pl.ds(z, 1), :] = tin0[z, R - 1:R, :]
         return carry
 
-    lax.fori_loop(0, Z, pack_tin, 0, unroll=4)
+    lax.fori_loop(0, Z, pack_tin, 0, unroll=8)
 
     peers = ty - 1
     for ok, _ in pairs:
@@ -197,7 +197,7 @@
         rhi_s[1, pl.ds(z, 1), :] = jnp.concatenate([t[NI - 1, j][S - 1:S] for j in range(NJ)], 1)
         return pack_cols(z, [t[i, 0] for i in range(NI)], [t[i, NJ - 1] for i in range(NI)], acc)
 
-    store_cols(1, lax.fori_loop(0, ZF, k_layer, zeros(), unroll=4))
+    store_cols(1, lax.fori_loop(0, ZF, k_layer, zeros(), unroll=8))
     loads[2].wait()
 
     def g_layer(z, acc):
@@ -206,7 +206,7 @@
         return pack_cols(z, [tile(floor0, z, i, 0) for i in range(NI)],
                          [tile(floor0, z, i, NJ - 1) for i in range(NI)], acc)
 
-    store_cols(0, lax.fori_loop(0, ZF, g_layer, zeros(), unroll=4))
+    store_cols(0, lax.fori_loop(0, ZF, g_layer, zeros(), unroll=8))
     start_if(f0)
 
     def floor_layer(first, src, dst, z, top, bottom):
@@ -310,9 +310,9 @@
                              [t[i, NJ - 1] for i in range(NI)], acc)
 
         if e == 0:
-            store_cols(2, lax.fori_loop(0, ZF, body, zeros(), unroll=4))
+            store_cols(2, lax.fori_loop(0, ZF, body, zeros(), unroll=8))
         else:
-            lax.fori_loop(0, ZF, body, 0, unroll=4)
+            lax.fori_loop(0, ZF, body, 0, unroll=8)
 
     NH, NK = R // S, NYW // L
 

time: 35.5 us -> 34.3 us (0.966)
  Pallas kernels: 31.1 us -> 29.8 us
    pallas_call x1, Pallas kernels: 31.1 us -> 29.8 us  [local(): pl.pallas_call(functools.partial(kernel, n, ty), out_shape=OUT(tin_shape,...]
where the time goes in v3:
time: 34.3 us; the launch traced here: 34.2 us
  Pallas kernels  29.8 us (87%)
  local copies, waits for them, and re-layouts  3.68 us (11%)
  between operations  0.64 us (2%)
    pallas_call x1, Pallas kernels, local(): pl.pallas_call(functools.partial(kernel, n, ty), out_shape=OUT(tin_shape,...  29.8 us
    unnamed x2, local copies, waits for them, and re-layouts  3.68 us

profile of v3, /device:TPU:0, one launch (start us, length us, event | category | flops | bytes accessed | tf_op | source)
XLA Modules:
  0.0 34.2 jit_solution(14640654202704423465)
XLA Ops:
  0.6 29.8 %shard_map.77 = (f32[64,16,1024]{2,1,0:T(8,128)S(1)}, f32[48,64,256]{2,1,0:T(8,128)S(1)}) custom-call(f32[64,16,1024]{2,1,0:T(8,128)} %tin_h.1, s32[64,16,1024]{2,1,0:T(8,128)} %flow_h.1, f32[2,64]{1,0:T(2,128)} %speeds_h.1, f32[48,64,256]{2,1,0:T(8,128)} %bitcast.4, s32[48,64,256]{2,1,0:T(8,128)} %bitcast.5, f32[3]{0:T(128)} %cond_h.1), custom_call_target="tpu_custom_call" | custom-call | flops 120000000 | bytes 23000000 | tf_op jit(solution)/shard_map/pallas_call | solution.py:432
  30.5 2.0 %copy.10 = f32[64,16,1024]{2,1,0:T(8,128)} copy(f32[64,16,1024]{2,1,0:T(8,128)S(1)} %get-tuple-element.6) | data formatting | bytes 8388608
  32.5 1.7 %copy.11 = f32[1,48,64,256]{3,2,1,0:T(8,128)} copy(f32[1,48,64,256]{3,2,1,0:T(8,128)S(1)} %bitcast.3) | data formatting | bytes 6291456
